TPU v7x, 256 devices: a whole 4x4x8 slice. The times are simulated.
256 devices in a mesh: prow: 32 (over y, z), pcol: 8 (over x, core).
Axes of the slice: x: 4, y: 4, z: 8, core: 2. Of those that a mesh axis runs over, the one named last changes fastest.
Arguments:
- trailing: bfloat16 [32768, 16384], P('prow', 'pcol'), may hold values from -6 to 6
- panel_block: bfloat16 [32768, 128], P('prow', 'pcol'), may hold values from -0.25 to 0.25
- lower_inverse: float32 [128, 128], replicated, as said below
- pivot_pairs: int32 [128], replicated, may hold values from 128 to 32767, as said below
Outputs:
- updated: bfloat16 [32768, 16384], P('prow', 'pcol')
Inputs may be any that keep to these rules, and one draw needn't show every extreme that they name: `pivot_pairs`: the 128 values are distinct and all at least 128; both ends of the range occur. `lower_inverse`: unit lower triangular.
All inputs are finite; a program needn't handle non-finite values.
Results may differ from a plain program's by a relative error of at most 0.0043.
Values may be sent and summed in bfloat16 or wider, within the bound.
A program may use at most 64 MiB of HBM per device.

v0:
```python
import jax
import jax.numpy as jnp
from jax import lax
from jax.sharding import PartitionSpec as P


def broadcast(value, axis, source):
    kept = jnp.where(lax.axis_index(axis) == source, value, 0).astype(value.dtype)
    return lax.psum(kept, axis)


def shards(trailing, panel_block, lower_inverse, pivot_pairs):
    rows_dev = trailing.shape[0]
    width = lower_inverse.shape[0]
    row_procs = lax.axis_size("prow")
    my_row = lax.axis_index("prow")
    is_root = my_row == 0
    zero_value = jnp.zeros((), jnp.bfloat16)
    block_index = pivot_pairs // width
    owned_flag = block_index % row_procs == my_row
    local_index = block_index // row_procs * width + pivot_pairs % width
    safe_index = jnp.where(owned_flag, local_index, 0)
    owned_rows = jnp.where(owned_flag[:, None], trailing[safe_index], zero_value)
    top_local = trailing[:width]
    picked = lax.psum(owned_rows, "prow").astype(jnp.float32).astype(jnp.bfloat16)
    top_rows = broadcast(top_local, "prow", 0)
    target_index = jnp.where(owned_flag, local_index, rows_dev)
    swapped = trailing.at[target_index].set(top_rows, mode="drop")
    u_block = jnp.dot(
        lower_inverse, picked.astype(jnp.float32), precision=lax.Precision.HIGHEST
    ).astype(jnp.bfloat16)
    whole_panel = lax.all_gather(panel_block, "pcol", axis=1, tiled=True)
    product = jnp.dot(whole_panel, u_block, preferred_element_type=jnp.float32)
    updated = (swapped.astype(jnp.float32) - product).astype(jnp.bfloat16)
    head_rows = jnp.where(is_root, u_block, updated[:width])
    return jnp.concatenate([head_rows, updated[width:]], axis=0)


def solution(mesh):
    in_specs = (P("prow", "pcol"), P("prow", "pcol"), P(), P())
    out_specs = P("prow", "pcol")
    return jax.shard_map(shards, mesh=mesh, in_specs=in_specs, out_specs=out_specs, check_vma=False)
```

profile of v0, /device:TPU:2, one launch (start us, length us, event | category | flops | bytes accessed | tf_op | source)
XLA Modules:
  0.0 191.4 jit_solution(2317395671887024241)
XLA Ops:
  6.5 0.0 copy-start
  6.5 0.0 copy-start.3
  6.5 0.0 all-reduce.3.cloned.1.call-start
  6.5 4.8 %copy.9 = bf16[1024,2048]{1,0:T(8,128)(2,1)} copy(bf16[1024,2048]{1,0:T(8,128)(2,1)} %param.4) | data formatting | bytes 8388608
  11.4 0.0 copy-start.2
  11.4 0.0 copy-done.3
  11.4 4.2 %gather_fusion = bf16[128,2048]{1,0:T(8,128)(2,1)S(1)} fusion(bf16[1024,2048]{1,0:T(8,128)(2,1)} %copy.9, s32[1024]{0:T(1024)S(1)} %pad_clamp_fusion), kind=kCustom, calls=%fused_computation | custom fusion | bytes 1049088 | tf_op jit(solution)/shard_map/gather | solution.py:23
  15.6 2.2 %slice_select_fusion.1 = (bf16[128,2048]{1,0:T(8,128)(2,1)}, bf16[128,2048]{1,0:T(8,128)(2,1)}) fusion(bf16[1024,2048]{1,0:T(8,128)(2,1)} %copy.9, pred[]{:T(512)S(6)} %eq.13, bf16[128,2048]{1,0:T(8,128)(2,1)S(1)} %gather_fusion, pred[128]{0:T(512)(128)(4,1)S(1)} %get-tuple-element.9), kind=kLoop, calls=%fused_computation.7 | loop fusion | flops 524288 | bytes 2097281 | tf_op jit(solution)/shard_map/jit(_where)/select_n | solution.py:8
  17.8 0.0 all-reduce.3.cloned.1.call-update
  17.8 0.0 copy-done.2
  17.9 12.9 %all_gather.3 = bf16[1024,128]{0,1:T(8,128)(2,1)S(1)} all-gather(bf16[1024,16]{0,1:T(8,128)(2,1)S(1)} %copy-done.2), channel_id=1, replica_groups=mesh['prow'=32,'pcol'=8] {'pcol'}, dimensions={1}, use_global_device_ids=true | all-gather | bytes 294912 | tf_op jit(solution)/shard_map/all_gather | solution.py:32
  30.8 139.9 %all-reduce.3.cloned.1.call-done = (bf16[128,2048]{1,0:T(8,128)(2,1)}, bf16[128,2048]{1,0:T(8,128)(2,1)}) async-done(((bf16[128,2048]{1,0:T(8,128)(2,1)}, bf16[128,2048]{1,0:T(8,128)(2,1)}), (bf16[128,2048]{1,0:T(8,128)(2,1)}, bf16[128,2048]{1,0:T(8,128)(2,1)})) %all-reduce.3.cloned.1.call-update) | async-done | bytes 1048592 | tf_op jit(solution)/shard_map/psum | solution.py:9
  170.6 0.0 copy-start.1
  170.6 6.9 %scatter_fusion = bf16[1024,2048]{1,0:T(8,128)(2,1)} fusion(bf16[1024,2048]{1,0:T(8,128)(2,1)} %copy.9, s32[128]{0:T(128)S(1)} %compare_select_fusion, bf16[128,2048]{1,0:T(8,128)(2,1)} %get-tuple-element.5), kind=kCustom, calls=%fused_computation.1 | custom fusion | bytes 1573376 | tf_op jit(solution)/shard_map/scatter | solution.py:28
  177.6 0.0 copy-done
  177.6 0.0 copy-done.1
  177.6 0.6 convolution_convert_fusion
  178.2 3.5 %fusion = bf16[1024,2048]{1,0:T(8,128)(2,1)S(1)} fusion(bf16[1024,2048]{1,0:T(8,128)(2,1)} %scatter_fusion, bf16[2048,128]{0,1:T(8,128)(2,1)S(1)} %convolution_convert_fusion, bf16[1024,128]{0,1:T(8,128)(2,1)S(1)} %all_gather.3), kind=kOutput, calls=%fused_computation.3 | convolution fusion | flops 543162368 | bytes 9175040 | tf_op jit(solution)/shard_map/dot_general | solution.py:33
  181.6 0.1 slice_select_fusion
  181.7 0.3 slice.15
  182.0 2.5 %pad_maximum_fusion = bf16[1024,2048]{1,0:T(8,128)(2,1)} fusion(bf16[896,2048]{1,0:T(8,128)(2,1)S(1)} %slice.15, bf16[128,2048]{1,0:T(8,128)(2,1)S(1)} %slice_select_fusion), kind=kLoop, calls=%fused_computation.4 | loop fusion | flops 8388608 | bytes 8388608 | tf_op jit(solution)/shard_map/concatenate | solution.py:36
  (3 shorter events, 0.0 us)
Async XLA Ops:
  6.5 171.1 %copy-start = (f32[128,128]{1,0:T(8,128)S(1)}, f32[128,128]{1,0:T(8,128)}, u32[]{:S(2)}) copy-start(f32[128,128]{1,0:T(8,128)} %param.6) | copy-start | bytes 196612
  6.5 4.8 %copy-start.3 = (s32[128]{0:T(128)S(1)}, s32[128]{0:T(128)}, u32[]{:S(2)}) copy-start(s32[128]{0:T(128)} %param.7) | copy-start | bytes 1540
  6.5 164.1 %all-reduce.3.cloned.1.call-start = ((), (), s32[]{:S(2)}) async-start(), calls=%async_computation | async-start | bytes 2097152 | tf_op jit(solution)/shard_map/psum | solution.py:9
  11.4 6.5 %copy-start.2 = (bf16[1024,16]{0,1:T(8,128)(2,1)S(1)}, bf16[1024,16]{0,1:T(8,128)(2,1)}, u32[]{:S(2)}) copy-start(bf16[1024,16]{0,1:T(8,128)(2,1)} %param.5) | copy-start | bytes 98308
  170.6 6.9 %copy-start.1 = (bf16[128,2048]{1,0:T(8,128)(2,1)S(1)}, bf16[128,2048]{1,0:T(8,128)(2,1)}, u32[]{:S(2)}) copy-start(bf16[128,2048]{1,0:T(8,128)(2,1)} %get-tuple-element.6) | copy-start | bytes 1572868
Sparse Core Ops, SparseCore 0:
  18.0 152.6 all-reduce.2
where the time goes:
time: 192 us; the launch traced here: 191 us
  waiting for transfers between devices  140 us (73%)
  local copies, waits for them, and re-layouts  16.2 us (8%)
  between operations  13.5 us (7%)
  blocking collectives  12.9 us (7%)
  other arithmetic  4.83 us (3%)
  matrix products  4.04 us (2%)
    psum x1, waiting for transfers between devices, broadcast(): return lax.psum(kept, axis)  140 us
    all_gather x1, blocking collectives, shards(): whole_panel = lax.all_gather(panel_block, 'pcol', axis=1, tiled=True)  12.9 us
    scatter x1, local copies, waits for them, and re-layouts, shards(): swapped = trailing.at[target_index].set(top_rows, mode='drop')  6.94 us
    unnamed x9, local copies, waits for them, and re-layouts  4.84 us
    gather x1, local copies, waits for them, and re-layouts, shards(): trailing[safe_index]  4.17 us
  transfers between devices with their start and end apart: 1, of which 1 were waited for; matrix products, arithmetic and copies ran while one was open for 0% of the time, Pallas kernels for 0%

commit v1 on v0

v1 whole, which is shorter than its diff:
```python
import functools

import jax
import jax.numpy as jnp
from jax import lax
from jax.experimental import pallas as pl
from jax.experimental.pallas import tpu as pltpu
from jax.sharding import PartitionSpec as P

MESH = pl.DeviceIdType.MESH
LANES = 128


def torus_of(procs):
    n_y = {32: 4, 8: 2}[procs]
    return n_y, procs // n_y


def near_first(n):
    return sorted(range(1, n), key=lambda k: (min(k, n - k), k))


def far_first(n):
    return sorted(range(n), key=lambda k: (-min(k, n - k), k))


def kernel(n_y, n_z, n_c, rows, cols, width,
           trailing_ref, panel_ref, inverse_ref, pivots_ref, out_ref,
           held, picked, from_y, summed, from_z, pieces, top_out, top_in, panels, left,
           panel_held, inverse_held, pivots_held, small_sem, load_sem, ry_send, ry_recv, rz_send, rz_recv, top_send, top_recv, spread_send, spread_recv,
           gz_send, gz_recv, gy_send, gy_recv, panel_send, panel_recv):
    procs = n_y * n_z
    n_j = n_z // 2
    half = width // 2
    group = cols // n_y
    me = lax.axis_index("prow")
    c = lax.axis_index("pcol")
    y, z = me // n_z, me % n_z
    j_own, h_own = z // 2, z % 2
    is_root = me == 0

    def y_peer(k):
        return (y + k) % n_y

    def z_peer(k):
        return (z + k) % n_z

    def send(src, dst, send_sem, recv_sem, row, col):
        copy = pltpu.make_async_remote_copy(
            src_ref=src, dst_ref=dst, send_sem=send_sem, recv_sem=recv_sem,
            device_id=(row, col), device_id_type=MESH,
        )
        copy.start()
        return copy

    def arrived(dst, recv_sem):
        pltpu.make_async_remote_copy(
            src_ref=dst, dst_ref=dst, send_sem=recv_sem, recv_sem=recv_sem,
            device_id=(me, c), device_id_type=MESH,
        ).wait_recv()

    barrier = pltpu.get_barrier_semaphore()
    for k in range(1, n_y):
        pl.semaphore_signal(barrier, inc=1, device_id=(y_peer(k) * n_z + z, c), device_id_type=MESH)
    for k in range(1, n_z):
        pl.semaphore_signal(barrier, inc=1, device_id=(y * n_z + z_peer(k), c), device_id_type=MESH)
    for k in range(1, n_c):
        pl.semaphore_signal(barrier, inc=1, device_id=(me, (c + k) % n_c), device_id_type=MESH)

    small = [
        pltpu.make_async_copy(pivots_ref, pivots_held, small_sem.at[0]),
        pltpu.make_async_copy(panel_ref, panel_held, small_sem.at[1]),
        pltpu.make_async_copy(inverse_ref, inverse_held, small_sem.at[2]),
    ]
    for copy in small:
        copy.start()

    y_order = list(range(1, n_y)) + [0]
    loads = []
    for k in y_order:
        span = pl.ds(pl.multiple_of(y_peer(k) * group, group), group)
        load = pltpu.make_async_copy(trailing_ref.at[:, span], held.at[:, span], load_sem.at[k])
        load.start()
        loads.append(load)

    small[0].wait()
    pivots = pivots_held[...]
    block = pivots // width
    where = jnp.where(block % procs == me, block // procs * width + pivots % width, -1)
    where = where.astype(jnp.float32)
    spread = jnp.broadcast_to(where, (width, width)).T
    for b in range(rows // LANES):
        row = lax.broadcasted_iota(jnp.int32, (width, LANES), 1) + b * LANES
        select = (spread == row.astype(jnp.float32)).astype(jnp.bfloat16)
        left[width:2 * width, b * LANES:(b + 1) * LANES] = select

    for n, k in enumerate(y_order):
        loads[n].wait()
        yk = y_peer(k)
        span = pl.ds(pl.multiple_of(yk * group, group), group)
        rows_out = jnp.dot(left[width:2 * width, :], held[:, span], preferred_element_type=jnp.float32)
        rows_out = rows_out.astype(jnp.bfloat16)
        for j in range(n_j):
            picked[yk, j] = rows_out[:, j * LANES:(j + 1) * LANES]

    @pl.when(is_root)
    def _():
        for k in range(n_z):
            for q in range(n_y):
                at = (q * n_j + k // 2) * LANES
                top_out[k, q] = held[(k % 2) * half:(k % 2 + 1) * half, at:at + LANES]

    pl.semaphore_wait(barrier, n_y - 1 + n_z - 1 + n_c - 1)

    @pl.when(is_root)
    def _():
        copies = []
        for k in range(1, n_z):
            copies.append(send(top_out.at[k], top_in, top_send.at[k], top_recv.at[0], k, c))
        top_in[...] = top_out[0]

    j_order = [m for m in far_first(n_j)]
    ry_copies = []
    for m in j_order:
        j = (j_own + m) % n_j
        for k in range(1, n_y):
            yk = y_peer(k)
            ry_copies.append(send(picked.at[yk, j], from_y.at[j, k], ry_send.at[m, k], ry_recv.at[j, k],
                                  yk * n_z + z, c))

    small[1].wait()
    panel_copies = []
    for k in range(1, n_c):
        ck = (c + k) % n_c
        panel_copies.append(send(panel_held, panels.at[c], panel_send.at[k], panel_recv.at[k], me, ck))
    panels[c] = panel_held[...]

    rz_copies = []
    for m in j_order:
        j = (j_own + m) % n_j
        for k in range(1, n_y):
            arrived(from_y.at[j, k], ry_recv.at[j, k])
        total = picked[y, j]
        for k in range(1, n_y):
            total = total + from_y[j, k]
        summed[j] = total
        if m == 0:
            zk = j * 2 + 1 - h_own
            rz_copies.append(send(summed.at[j], from_z.at[z], rz_send.at[0], rz_recv.at[z], y * n_z + zk, c))
        else:
            for h in range(2):
                zk = j * 2 + h
                rz_copies.append(send(summed.at[j], from_z.at[z], rz_send.at[m * 2 + h], rz_recv.at[z],
                                      y * n_z + zk, c))

    @pl.when(y == 0)
    def _():
        @pl.when(z != 0)
        def _():
            arrived(top_in, top_recv.at[0])
        for k in range(1, n_y):
            send(top_in.at[k], pieces.at[k * n_z + z, 1], spread_send.at[k], spread_recv.at[0], k * n_z + z, c)
        pieces[me, 1] = top_in[0]

    for k in range(1, n_c):
        ck = (c + n_c - k) % n_c
        arrived(panels.at[ck], panel_recv.at[k])
    share = width // n_c
    for k in range(n_c):
        left[k * share:(k + 1) * share, :] = -panels[k]

    @pl.when(is_root)
    def _():
        row = lax.broadcasted_iota(jnp.int32, (width, width), 0)
        col = lax.broadcasted_iota(jnp.int32, (width, width), 1)
        left[0:width, 0:width] = (row == col).astype(jnp.bfloat16)

    tile = LANES

    def mask(b, carry):
        span = pl.ds(pl.multiple_of(b * tile, tile), tile)
        hit = jnp.sum(left[width:2 * width, span].astype(jnp.float32), axis=0, keepdims=True)
        hit = jnp.where(jnp.logical_and(is_root, b == 0), 1.0, hit)
        keep = (1.0 - jnp.broadcast_to(hit, (tile, tile))).T
        keep = keep.astype(jnp.bfloat16)
        for g in range(cols // LANES):
            part = pl.ds(g * LANES, LANES)
            held[span, part] = held[span, part] * keep
        return carry

    lax.fori_loop(0, rows // tile, mask, 0)

    total = summed[j_own]
    for k in near_first(n_z):
        zk = z_peer(k)
        arrived(from_z.at[zk], rz_recv.at[zk])
        total = total + from_z[zk]
    small[2].wait()
    inverse = inverse_held[pl.ds(pl.multiple_of(h_own * half, half), half), :]
    u = jnp.dot(inverse, total.astype(jnp.float32), precision=lax.Precision.HIGHEST,
                preferred_element_type=jnp.float32)
    pieces[me, 0] = u.astype(jnp.bfloat16)

    @pl.when(y != 0)
    def _():
        arrived(pieces.at[me, 1], spread_recv.at[0])

    gz_copies, gy_copies = [], []
    for k in near_first(n_z)[::-1]:
        gz_copies.append(send(pieces.at[me], pieces.at[me], gz_send.at[k], gz_recv.at[z], y * n_z + z_peer(k), c))
    for kz in [0] + near_first(n_z):
        zk = z_peer(kz)
        slot = y * n_z + zk
        if kz:
            arrived(pieces.at[slot], gz_recv.at[zk])
        for k in range(1, n_y):
            gy_copies.append(send(pieces.at[slot], pieces.at[slot], gy_send.at[kz, k], gy_recv.at[slot],
                                  y_peer(k) * n_z + z, c))

    for k in range(n_y):
        yk = y_peer(k)
        for pair in range(n_j // 2):
            base = yk * n_z + pair * 4
            if k:
                for q in range(4):
                    arrived(pieces.at[base + q], gy_recv.at[base + q])
            right = jnp.concatenate([
                jnp.concatenate([pieces[base + 0, part], pieces[base + 1, part]], axis=0)
                for part in range(2)
            ], axis=0)
            right_2 = jnp.concatenate([
                jnp.concatenate([pieces[base + 2, part], pieces[base + 3, part]], axis=0)
                for part in range(2)
            ], axis=0)
            right = jnp.concatenate([right, right_2], axis=1)
            span = pl.ds(pl.multiple_of((yk * n_j + pair * 2) * LANES, 2 * LANES), 2 * LANES)
            term = lax.dot_general(left[...], right, (((0,), (0,)), ((), ())),
                                   preferred_element_type=jnp.float32)
            out_ref[:, span] = (held[:, span].astype(jnp.float32) + term).astype(jnp.bfloat16)

    for copy in ry_copies + panel_copies + rz_copies + gz_copies + gy_copies:
        copy.wait_send()

    @pl.when(is_root)
    def _():
        for k in range(1, n_z):
            pltpu.make_async_remote_copy(
                src_ref=top_out.at[k], dst_ref=top_in, send_sem=top_send.at[k], recv_sem=top_recv.at[0],
                device_id=(k, c), device_id_type=MESH).wait_send()

    @pl.when(y == 0)
    def _():
        for k in range(1, n_y):
            pltpu.make_async_remote_copy(
                src_ref=top_in.at[k], dst_ref=pieces.at[k * n_z + z, 1], send_sem=spread_send.at[k],
                recv_sem=spread_recv.at[0], device_id=(k * n_z + z, c), device_id_type=MESH).wait_send()


def shards(trailing, panel_block, lower_inverse, pivot_pairs):
    rows, cols = trailing.shape
    width = lower_inverse.shape[0]
    procs, n_c = lax.axis_size("prow"), lax.axis_size("pcol")
    n_y, n_z = torus_of(procs)
    n_j, half, share = n_z // 2, width // 2, width // n_c
    bf16 = jnp.bfloat16
    dma = pltpu.SemaphoreType.DMA
    vmem = pl.BlockSpec(memory_space=pltpu.VMEM)
    return pl.pallas_call(
        functools.partial(kernel, n_y, n_z, n_c, rows, cols, width),
        out_shape=pltpu.VMEM((rows, cols), bf16),
        in_specs=[pl.BlockSpec(memory_space=pltpu.HBM)] * 4,
        out_specs=vmem,
        scratch_shapes=[
            pltpu.VMEM((rows, cols), bf16),
            pltpu.VMEM((n_y, n_j, width, LANES), bf16),
            pltpu.VMEM((n_j, n_y, width, LANES), bf16),
            pltpu.VMEM((n_j, width, LANES), bf16),
            pltpu.VMEM((n_z, width, LANES), bf16),
            pltpu.VMEM((procs, 2, half, LANES), bf16),
            pltpu.VMEM((n_z, n_y, half, LANES), bf16),
            pltpu.VMEM((n_y, half, LANES), bf16),
            pltpu.VMEM((n_c, share, rows), bf16),
            pltpu.VMEM((2 * width, rows), bf16),
            pltpu.VMEM((share, rows), bf16),
            pltpu.VMEM((width, width), jnp.float32),
            pltpu.VMEM((1, width), jnp.int32),
            dma((3,)), dma((n_y,)), dma((n_j, n_y)), dma((n_j, n_y)), dma((n_z,)), dma((n_z,)),
            dma((n_z,)), dma((1,)), dma((n_y,)), dma((1,)),
            dma((n_z,)), dma((n_z,)), dma((n_z, n_y)), dma((procs,)), dma((n_c,)), dma((n_c,)),
        ],
        compiler_params=pltpu.CompilerParams(
            collective_id=0, has_side_effects=True, vmem_limit_bytes=32 * 1024 * 1024
        ),
        name="lu_update",
    )(*(
        pltpu.with_memory_space_constraint(value, pltpu.HBM)
        for value in (trailing, panel_block.T, lower_inverse, pivot_pairs.reshape(1, width))
    ))


def solution(mesh):
    in_specs = (P("prow", "pcol"), P("prow", "pcol"), P(), P())
    out_specs = P("prow", "pcol")
    return jax.shard_map(shards, mesh=mesh, in_specs=in_specs, out_specs=out_specs, check_vma=False)
```

time: 192 us -> 44.2 us (0.23)
  the two profiles are of different devices: /device:TPU:2 before, /device:TPU:1 now
where the time goes in v1:
time: 44.2 us
  Pallas kernels  42.1 us (95%)
  local copies, waits for them, and re-layouts  2.02 us (5%)
    pallas_call x1, Pallas kernels, shards(): pl.pallas_call(functools.partial(kernel, n_y, n_z, n_c, rows, cols, width...  42.1 us
    unnamed x1, local copies, waits for them, and re-layouts  2.02 us

profile of v1, /device:TPU:1, one launch (start us, length us, event | category | flops | bytes accessed | tf_op | source)
XLA Modules:
  0.0 44.2 jit_solution(14489124986137355084)
XLA Ops:
  0.0 42.1 %lu_update.1 = bf16[1024,2048]{1,0:T(8,128)(2,1)S(1)} custom-call(bf16[1024,2048]{1,0:T(8,128)(2,1)} %trailing_ref.1, bf16[16,1024]{1,0:T(8,128)(2,1)} %bitcast.2, f32[128,128]{1,0:T(8,128)} %inverse_ref.1, s32[1,128]{1,0:T(1,128)} %bitcast.3), custom_call_target="tpu_custom_call" | custom-call | tf_op jit(solution)/shard_map/lu_update/pallas_call | solution.py:268
  42.1 2.0 %copy.6 = bf16[1024,2048]{1,0:T(8,128)(2,1)} copy(bf16[1024,2048]{1,0:T(8,128)(2,1)S(1)} %lu_update.1) | data formatting | bytes 8388608

commit v2 on v1

v2 whole, which is shorter than its diff:
```python
import functools

import jax
import jax.numpy as jnp
from jax import lax
from jax.experimental import pallas as pl
from jax.experimental.pallas import tpu as pltpu
from jax.sharding import PartitionSpec as P

MESH = pl.DeviceIdType.MESH
LANES = 128


def torus_of(procs):
    n_y = {32: 4, 8: 2}[procs]
    return n_y, procs // n_y


def near_first(n):
    return sorted(range(1, n), key=lambda k: (min(k, n - k), k))


def far_first(n):
    return sorted(range(n), key=lambda k: (-min(k, n - k), k))


def kernel(n_y, n_z, n_c, rows, cols, width,
           trailing_ref, panel_ref, inverse_ref, pivots_ref, held, left, right,
           select, picked, from_y, summed, from_z, u_all, top_all, top_out, top_in, panels,
           panel_held, inverse_held, pivots_held,
           small_sem, load_sem, ry_send, ry_recv, rz_send, rz_recv, top_send, top_recv, spread_send, spread_recv,
           uz_send, uz_recv, uy_send, uy_recv, tz_send, tz_recv, ty_send, ty_recv, panel_send, panel_recv):
    procs = n_y * n_z
    n_j = n_z // 2
    half = width // 2
    group = cols // n_y
    share = width // n_c
    me = lax.axis_index("prow")
    c = lax.axis_index("pcol")
    y, z = me // n_z, me % n_z
    j_own, h_own = z // 2, z % 2
    is_root = me == 0
    bf16 = jnp.bfloat16

    def y_peer(k):
        return (y + k) % n_y

    def z_peer(k):
        return (z + k) % n_z

    def remote(src, dst, send_sem, recv_sem, row, col):
        return pltpu.make_async_remote_copy(
            src_ref=src, dst_ref=dst, send_sem=send_sem, recv_sem=recv_sem,
            device_id=(row, col), device_id_type=MESH,
        )

    sent = []

    def send(*what):
        copy = remote(*what)
        copy.start()
        sent.append(copy)

    def arrived(dst, recv_sem):
        remote(dst, dst, recv_sem, recv_sem, me, c).wait_recv()

    barrier = pltpu.get_barrier_semaphore()
    for k in far_first(n_z)[:-1]:
        pl.semaphore_signal(barrier, inc=1, device_id=(y * n_z + z_peer(k), c), device_id_type=MESH)
    for k in far_first(n_y)[:-1]:
        pl.semaphore_signal(barrier, inc=1, device_id=(y_peer(k) * n_z + z, c), device_id_type=MESH)
    for k in range(1, n_c):
        pl.semaphore_signal(barrier, inc=1, device_id=(me, (c + k) % n_c), device_id_type=MESH)

    small = [
        pltpu.make_async_copy(pivots_ref, pivots_held, small_sem.at[0]),
        pltpu.make_async_copy(panel_ref, panel_held, small_sem.at[1]),
        pltpu.make_async_copy(inverse_ref, inverse_held, small_sem.at[2]),
    ]
    small[0].start()

    y_order = far_first(n_y)
    loads = []
    for k in y_order:
        span = pl.ds(pl.multiple_of(y_peer(k) * group, group), group)
        load = pltpu.make_async_copy(trailing_ref.at[:, span], held.at[:, span], load_sem.at[k])
        load.start()
        loads.append(load)
    small[1].start()
    small[2].start()

    small[0].wait()
    pivots = pivots_held[...]
    block = pivots // width
    where = jnp.where(block % procs == me, block // procs * width + pivots % width, -1)
    spread = jnp.broadcast_to(where.astype(jnp.float32), (width, width)).T
    for b in range(rows // LANES):
        row = lax.broadcasted_iota(jnp.int32, (width, LANES), 1) + b * LANES
        select[:, b * LANES:(b + 1) * LANES] = (spread == row.astype(jnp.float32)).astype(bf16)

    j_order = far_first(n_j)
    for n, k in enumerate(y_order):
        loads[n].wait()
        yk = y_peer(k)
        span = pl.ds(pl.multiple_of(yk * group, group), group)
        found = jnp.dot(select[...], held[:, span], preferred_element_type=jnp.float32).astype(bf16)
        for j in range(n_j):
            picked[yk, j] = found[:, j * LANES:(j + 1) * LANES]

    @pl.when(is_root)
    def _():
        for k in far_first(n_z):
            for q in range(n_y):
                at = (q * n_j + k // 2) * LANES
                top_out[k, q] = held[(k % 2) * half:(k % 2 + 1) * half, at:at + LANES]
        top_in[...] = top_out[0]

    pl.semaphore_wait(barrier, n_y - 1 + n_z - 1 + n_c - 1)

    @pl.when(is_root)
    def _():
        for k in far_first(n_z)[:-1]:
            remote(top_out.at[k], top_in, top_send.at[k], top_recv.at[0], k, c).start()

    for m in j_order:
        j = (j_own + m) % n_j
        for k in far_first(n_y)[:-1]:
            yk = y_peer(k)
            send(picked.at[yk, j], from_y.at[j, k], ry_send.at[m, k], ry_recv.at[j, k], yk * n_z + z, c)

    small[1].wait()
    for k in range(1, n_c):
        ck = (c + k) % n_c
        send(panel_held, panels.at[c], panel_send.at[k], panel_recv.at[k], me, ck)
    panels[c] = panel_held[...]

    def spread_z(ref, send_sems, recv_sems):
        for k in near_first(n_z):
            send(ref.at[me], ref.at[me], send_sems.at[k], recv_sems.at[z], y * n_z + z_peer(k), c)

    def hand_on(ref, send_sems, recv_sems, kz):
        slot = y * n_z + z_peer(kz)
        for k in far_first(n_y)[:-1]:
            send(ref.at[slot], ref.at[slot], send_sems.at[kz, k], recv_sems.at[slot], y_peer(k) * n_z + z, c)

    def hand_on_all(ref, z_sems, send_sems, recv_sems):
        for kz in near_first(n_z):
            zk = z_peer(kz)
            arrived(ref.at[y * n_z + zk], z_sems.at[zk])
            hand_on(ref, send_sems, recv_sems, kz)

    def top_along_y():
        @pl.when(y == 0)
        def _():
            @pl.when(z != 0)
            def _():
                arrived(top_in, top_recv.at[0])
            for k in far_first(n_y)[:-1]:
                remote(top_in.at[k], top_all.at[k * n_z + z], spread_send.at[k], spread_recv.at[0],
                       k * n_z + z, c).start()
            top_all[me] = top_in[0]

    for m in j_order:
        j = (j_own + m) % n_j
        for k in range(1, n_y):
            arrived(from_y.at[j, k], ry_recv.at[j, k])
        total = picked[y, j]
        for k in range(1, n_y):
            total = total + from_y[j, k]
        summed[j] = total
        for h in range(2) if m else range(1):
            zk = j * 2 + h if m else j * 2 + 1 - h_own
            send(summed.at[j], from_z.at[z], rz_send.at[m * 2 + h], rz_recv.at[z], y * n_z + zk, c)
        if m == j_order[1]:
            top_along_y()

    tile = LANES

    def mask(b, carry):
        span = pl.ds(pl.multiple_of(b * tile, tile), tile)
        row = lax.broadcasted_iota(jnp.int32, (tile, width), 0) + b * tile
        hit = (where == row).astype(jnp.float32)
        left[span, width:2 * width] = hit.astype(bf16)
        hit = jnp.sum(hit, axis=1, keepdims=True)
        hit = jnp.where(jnp.logical_and(is_root, b == 0), 1.0, hit)
        keep = jnp.broadcast_to(1.0 - hit, (tile, LANES)).astype(bf16)
        for g in range(cols // LANES):
            part = pl.ds(g * LANES, LANES)
            held[span, part] = held[span, part] * keep
        return carry

    lax.fori_loop(0, rows // tile, mask, 0)

    @pl.when(y != 0)
    def _():
        arrived(top_all.at[me], spread_recv.at[0])

    spread_z(top_all, tz_send, tz_recv)
    hand_on(top_all, ty_send, ty_recv, 0)

    small[2].wait()
    inverse = inverse_held[pl.ds(pl.multiple_of(h_own * half, half), half), :]
    total = summed[j_own]
    for k in near_first(n_z):
        zk = z_peer(k)
        arrived(from_z.at[zk], rz_recv.at[zk])
        total = total + from_z[zk]
    u = jnp.dot(inverse, total.astype(jnp.float32), precision=lax.Precision.HIGHEST,
                preferred_element_type=jnp.float32)
    u_all[me] = u.astype(bf16)

    spread_z(u_all, uz_send, uz_recv)
    hand_on(u_all, uy_send, uy_recv, 0)
    hand_on_all(top_all, tz_recv, ty_send, ty_recv)

    for k in range(1, n_c):
        arrived(panels.at[(c + n_c - k) % n_c], panel_recv.at[k])
    whole = jnp.concatenate([panels[k] for k in range(n_c)], axis=0)
    left[:, 0:width] = -whole.astype(jnp.float32).T.astype(bf16)

    @pl.when(is_root)
    def _():
        row = lax.broadcasted_iota(jnp.int32, (width, width), 0)
        col = lax.broadcasted_iota(jnp.int32, (width, width), 1)
        left[0:width, 0:width] = (row == col).astype(bf16)

    hand_on_all(u_all, uz_recv, uy_send, uy_recv)

    for k in range(n_y):
        yk = y_peer(k)
        for j in range(n_j):
            span = pl.ds(pl.multiple_of((yk * n_j + j) * LANES, LANES), LANES)
            for h in range(2):
                slot = yk * n_z + j * 2 + h
                if k:
                    arrived(top_all.at[slot], ty_recv.at[slot])
                right[width + h * half:width + (h + 1) * half, span] = top_all[slot]
    for k in range(n_y):
        yk = y_peer(k)
        for j in range(n_j):
            span = pl.ds(pl.multiple_of((yk * n_j + j) * LANES, LANES), LANES)
            for h in range(2):
                slot = yk * n_z + j * 2 + h
                if k:
                    arrived(u_all.at[slot], uy_recv.at[slot])
                right[h * half:(h + 1) * half, span] = u_all[slot]

    for copy in sent:
        copy.wait_send()

    @pl.when(is_root)
    def _():
        for k in range(1, n_z):
            remote(top_out.at[k], top_in, top_send.at[k], top_recv.at[0], k, c).wait_send()

    @pl.when(y == 0)
    def _():
        for k in range(1, n_y):
            remote(top_in.at[k], top_all.at[k * n_z + z], spread_send.at[k], spread_recv.at[0],
                   k * n_z + z, c).wait_send()


def update(parts, held, left, right, out_ref, done, sems):
    step = held.shape[1] // parts
    for n in range(parts):
        span = slice(n * step, (n + 1) * step)
        term = jnp.dot(left[...], right[:, span], preferred_element_type=jnp.float32)
        done[n] = (held[:, span].astype(jnp.float32) + term).astype(jnp.bfloat16)
        pltpu.make_async_copy(done.at[n], out_ref.at[:, span], sems.at[n]).start()
    for n in range(parts):
        span = slice(n * step, (n + 1) * step)
        pltpu.make_async_copy(done.at[n], out_ref.at[:, span], sems.at[n]).wait()


def shards(trailing, panel_block, lower_inverse, pivot_pairs):
    rows, cols = trailing.shape
    width = lower_inverse.shape[0]
    procs, n_c = lax.axis_size("prow"), lax.axis_size("pcol")
    n_y, n_z = torus_of(procs)
    n_j, half, share = n_z // 2, width // 2, width // n_c
    bf16 = jnp.bfloat16
    dma = pltpu.SemaphoreType.DMA
    vmem = pl.BlockSpec(memory_space=pltpu.VMEM)
    factors = pl.pallas_call(
        functools.partial(kernel, n_y, n_z, n_c, rows, cols, width),
        out_shape=[
            pltpu.VMEM((rows, cols), bf16), pltpu.VMEM((rows, 2 * width), bf16), pltpu.VMEM((2 * width, cols), bf16)
        ],
        in_specs=[pl.BlockSpec(memory_space=pltpu.HBM)] * 4,
        out_specs=[vmem] * 3,
        scratch_shapes=[
            pltpu.VMEM((width, rows), bf16),
            pltpu.VMEM((n_y, n_j, width, LANES), bf16),
            pltpu.VMEM((n_j, n_y, width, LANES), bf16),
            pltpu.VMEM((n_j, width, LANES), bf16),
            pltpu.VMEM((n_z, width, LANES), bf16),
            pltpu.VMEM((procs, half, LANES), bf16),
            pltpu.VMEM((procs, half, LANES), bf16),
            pltpu.VMEM((n_z, n_y, half, LANES), bf16),
            pltpu.VMEM((n_y, half, LANES), bf16),
            pltpu.VMEM((n_c, share, rows), bf16),
            pltpu.VMEM((share, rows), bf16),
            pltpu.VMEM((width, width), jnp.float32),
            pltpu.VMEM((1, width), jnp.int32),
            dma((3,)), dma((n_y,)), dma((n_j, n_y)), dma((n_j, n_y)), dma((n_z,)), dma((n_z,)),
            dma((n_z,)), dma((1,)), dma((n_y,)), dma((1,)),
            dma((n_z,)), dma((n_z,)), dma((n_z, n_y)), dma((procs,)),
            dma((n_z,)), dma((n_z,)), dma((n_z, n_y)), dma((procs,)), dma((n_c,)), dma((n_c,)),
        ],
        compiler_params=pltpu.CompilerParams(
            collective_id=0, has_side_effects=True, vmem_limit_bytes=32 * 1024 * 1024
        ),
        name="exchange",
    )(*(
        pltpu.with_memory_space_constraint(value, pltpu.HBM)
        for value in (trailing, panel_block.T, lower_inverse, pivot_pairs.reshape(1, width))
    ))
    parts = cols // (2 * LANES)
    return pl.pallas_call(
        functools.partial(update, parts),
        out_shape=jax.ShapeDtypeStruct((rows, cols), bf16),
        in_specs=[vmem] * 3,
        out_specs=pl.BlockSpec(memory_space=pltpu.HBM),
        scratch_shapes=[pltpu.VMEM((parts, rows, cols // parts), bf16), dma((parts,))],
        compiler_params=pltpu.CompilerParams(vmem_limit_bytes=32 * 1024 * 1024),
        name="update",
    )(*(pltpu.with_memory_space_constraint(value, pltpu.VMEM) for value in factors))


def solution(mesh):
    in_specs = (P("prow", "pcol"), P("prow", "pcol"), P(), P())
    out_specs = P("prow", "pcol")
    return jax.shard_map(shards, mesh=mesh, in_specs=in_specs, out_specs=out_specs, check_vma=False)
```

time: 44.2 us -> 38 us (0.86)
  the two profiles are of different devices: /device:TPU:1 before, /device:TPU:2 now
where the time goes in v2:
time: 38 us; the launch traced here: 37.9 us
  Pallas kernels  37.9 us (100%)
    pallas_call x1, Pallas kernels, shards(): pl.pallas_call(functools.partial(kernel, n_y, n_z, n_c, rows, cols, width...  35.4 us
    pallas_call x1, Pallas kernels, shards(): pl.pallas_call(functools.partial(update, parts), out_shape=jax.ShapeDtype...  2.51 us

profile of v2, /device:TPU:2, one launch (start us, length us, event | category | flops | bytes accessed | tf_op | source)
XLA Modules:
  0.0 37.9 jit_solution(7308088618205624137)
XLA Ops:
  0.0 35.4 %exchange.1 = (bf16[1024,2048]{1,0:T(8,128)(2,1)S(1)}, bf16[1024,256]{1,0:T(8,128)(2,1)S(1)}, bf16[256,2048]{1,0:T(8,128)(2,1)S(1)}) custom-call(bf16[1024,2048]{1,0:T(8,128)(2,1)} %trailing_ref.1, bf16[16,1024]{1,0:T(8,128)(2,1)} %bitcast.2, f32[128,128]{1,0:T(8,128)} %inverse_ref.1, s32[1,128]{1,0:T(1,128)} %bitcast.3), custom_call_target="tpu_custom_call" | custom-call | tf_op jit(solution)/shard_map/exchange/pallas_call | solution.py:284
  35.4 2.5 %update.1 = bf16[1024,2048]{1,0:T(8,128)(2,1)} custom-call(bf16[1024,2048]{1,0:T(8,128)(2,1)S(1)} %get-tuple-element.8.held, bf16[1024,256]{1,0:T(8,128)(2,1)S(1)} %get-tuple-element.9.left, bf16[256,2048]{1,0:T(8,128)(2,1)S(1)} %get-tuple-element.10.right), custom_call_target="tpu_custom_call" | custom-call | tf_op jit(solution)/shard_map/update/pallas_call | solution.py:319

commit v3 on v2

--- a/solution.py
+++ b/solution.py
@@ -32,13 +32,13 @@
            uz_send, uz_recv, uy_send, uy_recv, tz_send, tz_recv, ty_send, ty_recv, panel_send, panel_recv):
     procs = n_y * n_z
     n_j = n_z // 2
-    half = width // 2
     group = cols // n_y
     share = width // n_c
     me = lax.axis_index("prow")
     c = lax.axis_index("pcol")
     y, z = me // n_z, me % n_z
-    j_own, h_own = z // 2, z % 2
+    j_own, collects = z // 2, z % 2 == 0
+    mine = y * n_j + j_own
     is_root = me == 0
     bf16 = jnp.bfloat16
 
@@ -109,18 +109,21 @@
 
     @pl.when(is_root)
     def _():
-        for k in far_first(n_z):
+        for j in far_first(n_j):
             for q in range(n_y):
-                at = (q * n_j + k // 2) * LANES
-                top_out[k, q] = held[(k % 2) * half:(k % 2 + 1) * half, at:at + LANES]
+                at = (q * n_j + j) * LANES
+                top_out[j, q] = held[0:width, at:at + LANES]
         top_in[...] = top_out[0]
 
     pl.semaphore_wait(barrier, n_y - 1 + n_z - 1 + n_c - 1)
 
+    def top_along_z(j):
+        return remote(top_out.at[j], top_in, top_send.at[j], top_recv.at[0], j * 2, c)
+
     @pl.when(is_root)
     def _():
-        for k in far_first(n_z)[:-1]:
-            remote(top_out.at[k], top_in, top_send.at[k], top_recv.at[0], k, c).start()
+        for j in far_first(n_j)[:-1]:
+            top_along_z(j).start()
 
     for m in j_order:
         j = (j_own + m) % n_j
@@ -149,16 +152,21 @@
             arrived(ref.at[y * n_z + zk], z_sems.at[zk])
             hand_on(ref, send_sems, recv_sems, kz)
 
-    def top_along_y():
-        @pl.when(y == 0)
+    def top_along_y(k):
+        return remote(top_in.at[k], top_all.at[k * n_j + j_own], spread_send.at[k], spread_recv.at[0],
+                      k * n_z + z, c)
+
+    def pass_top_on():
+        @pl.when(z != 0)
         def _():
-            @pl.when(z != 0)
-            def _():
-                arrived(top_in, top_recv.at[0])
-            for k in far_first(n_y)[:-1]:
-                remote(top_in.at[k], top_all.at[k * n_z + z], spread_send.at[k], spread_recv.at[0],
-                       k * n_z + z, c).start()
-            top_all[me] = top_in[0]
+            arrived(top_in, top_recv.at[0])
+        for k in far_first(n_y)[:-1]:
+            top_along_y(k).start()
+        top_all[mine] = top_in[0]
+
+    def to_collector(m):
+        j = (j_own + m) % n_j
+        return remote(summed.at[j], from_z.at[z], rz_send.at[m], rz_recv.at[z], y * n_z + j * 2, c)
 
     for m in j_order:
         j = (j_own + m) % n_j
@@ -168,11 +176,37 @@
         for k in range(1, n_y):
             total = total + from_y[j, k]
         summed[j] = total
-        for h in range(2) if m else range(1):
-            zk = j * 2 + h if m else j * 2 + 1 - h_own
-            send(summed.at[j], from_z.at[z], rz_send.at[m * 2 + h], rz_recv.at[z], y * n_z + zk, c)
-        if m == j_order[1]:
-            top_along_y()
+        if m:
+            to_collector(m).start()
+        else:
+            pl.when(jnp.logical_not(collects))(lambda: to_collector(0).start())
+        if m == j_order[0]:
+            pl.when(jnp.logical_and(y == 0, collects))(pass_top_on)
+
+    def along_z(ref, send_sems, recv_sems, k):
+        return remote(ref.at[mine], ref.at[mine], send_sems.at[k], recv_sems.at[j_own], y * n_z + z_peer(k), c)
+
+    def spread_z(ref, send_sems, recv_sems):
+        for k in near_first(n_z):
+            along_z(ref, send_sems, recv_sems, k).start()
+
+    def hand_on(ref, send_sems, recv_sems, m):
+        slot = y * n_j + (j_own + m) % n_j
+        for k in far_first(n_y)[:-1]:
+            send(ref.at[slot], ref.at[slot], send_sems.at[m, k], recv_sems.at[slot], y_peer(k) * n_z + z, c)
+
+    def hand_on_all(ref, z_sems, send_sems, recv_sems, which):
+        for m in which:
+            j = (j_own + m) % n_j
+
+            def wait(j=j):
+                arrived(ref.at[y * n_j + j], z_sems.at[j])
+
+            if m:
+                wait()
+            else:
+                pl.when(jnp.logical_not(collects))(wait)
+            hand_on(ref, send_sems, recv_sems, m)
 
     tile = LANES
 
@@ -191,27 +225,29 @@
 
     lax.fori_loop(0, rows // tile, mask, 0)
 
-    @pl.when(y != 0)
-    def _():
-        arrived(top_all.at[me], spread_recv.at[0])
-
-    spread_z(top_all, tz_send, tz_recv)
-    hand_on(top_all, ty_send, ty_recv, 0)
+    @pl.when(collects)
+    def _():
+        @pl.when(y != 0)
+        def _():
+            arrived(top_all.at[mine], spread_recv.at[0])
+
+        spread_z(top_all, tz_send, tz_recv)
 
     small[2].wait()
-    inverse = inverse_held[pl.ds(pl.multiple_of(h_own * half, half), half), :]
-    total = summed[j_own]
-    for k in near_first(n_z):
-        zk = z_peer(k)
-        arrived(from_z.at[zk], rz_recv.at[zk])
-        total = total + from_z[zk]
-    u = jnp.dot(inverse, total.astype(jnp.float32), precision=lax.Precision.HIGHEST,
-                preferred_element_type=jnp.float32)
-    u_all[me] = u.astype(bf16)
-
-    spread_z(u_all, uz_send, uz_recv)
-    hand_on(u_all, uy_send, uy_recv, 0)
-    hand_on_all(top_all, tz_recv, ty_send, ty_recv)
+
+    @pl.when(collects)
+    def _():
+        total = summed[j_own]
+        for k in near_first(n_z):
+            zk = z_peer(k)
+            arrived(from_z.at[zk], rz_recv.at[zk])
+            total = total + from_z[zk]
+        u = jnp.dot(inverse_held[...], total.astype(jnp.float32), precision=lax.Precision.HIGHEST,
+                    preferred_element_type=jnp.float32)
+        u_all[mine] = u.astype(bf16)
+        spread_z(u_all, uz_send, uz_recv)
+
+    hand_on_all(top_all, tz_recv, ty_send, ty_recv, [0, 1])
 
     for k in range(1, n_c):
         arrived(panels.at[(c + n_c - k) % n_c], panel_recv.at[k])
@@ -224,40 +260,45 @@
         col = lax.broadcasted_iota(jnp.int32, (width, width), 1)
         left[0:width, 0:width] = (row == col).astype(bf16)
 
-    hand_on_all(u_all, uz_recv, uy_send, uy_recv)
-
-    for k in range(n_y):
-        yk = y_peer(k)
-        for j in range(n_j):
-            span = pl.ds(pl.multiple_of((yk * n_j + j) * LANES, LANES), LANES)
-            for h in range(2):
-                slot = yk * n_z + j * 2 + h
+    hand_on_all(u_all, uz_recv, uy_send, uy_recv, [0])
+    hand_on_all(top_all, tz_recv, ty_send, ty_recv, [3])
+    hand_on_all(u_all, uz_recv, uy_send, uy_recv, [1])
+    hand_on_all(top_all, tz_recv, ty_send, ty_recv, [2])
+    hand_on_all(u_all, uz_recv, uy_send, uy_recv, [3, 2])
+
+    finished = len(sent) - 3 * (n_y - 1)
+    for copy in sent[:finished]:
+        copy.wait_send()
+    for m in range(1, n_j):
+        to_collector(m).wait_send()
+    pl.when(jnp.logical_not(collects))(lambda: to_collector(0).wait_send())
+
+    for first, ref, sems in ((width, top_all, ty_recv), (0, u_all, uy_recv)):
+        for k in range(n_y):
+            for j in range(n_j):
+                slot = y_peer(k) * n_j + j
                 if k:
-                    arrived(top_all.at[slot], ty_recv.at[slot])
-                right[width + h * half:width + (h + 1) * half, span] = top_all[slot]
-    for k in range(n_y):
-        yk = y_peer(k)
-        for j in range(n_j):
-            span = pl.ds(pl.multiple_of((yk * n_j + j) * LANES, LANES), LANES)
-            for h in range(2):
-                slot = yk * n_z + j * 2 + h
-                if k:
-                    arrived(u_all.at[slot], uy_recv.at[slot])
-                right[h * half:(h + 1) * half, span] = u_all[slot]
-
-    for copy in sent:
+                    arrived(ref.at[slot], sems.at[slot])
+                right[first:first + width, pl.ds(pl.multiple_of(slot * LANES, LANES), LANES)] = ref[slot]
+
+    for copy in sent[finished:]:
         copy.wait_send()
 
+    @pl.when(collects)
+    def _():
+        for k in range(1, n_z):
+            along_z(top_all, tz_send, tz_recv, k).wait_send()
+            along_z(u_all, uz_send, uz_recv, k).wait_send()
+
     @pl.when(is_root)
     def _():
-        for k in range(1, n_z):
-            remote(top_out.at[k], top_in, top_send.at[k], top_recv.at[0], k, c).wait_send()
-
-    @pl.when(y == 0)
+        for j in range(1, n_j):
+            top_along_z(j).wait_send()
+
+    @pl.when(jnp.logical_and(y == 0, collects))
     def _():
         for k in range(1, n_y):
-            remote(top_in.at[k], top_all.at[k * n_z + z], spread_send.at[k], spread_recv.at[0],
-                   k * n_z + z, c).wait_send()
+            top_along_y(k).wait_send()
 
 
 def update(parts, held, left, right, out_ref, done, sems):
@@ -277,7 +318,7 @@
     width = lower_inverse.shape[0]
     procs, n_c = lax.axis_size("prow"), lax.axis_size("pcol")
     n_y, n_z = torus_of(procs)
-    n_j, half, share = n_z // 2, width // 2, width // n_c
+    n_j, share = n_z // 2, width // n_c
     bf16 = jnp.bfloat16
     dma = pltpu.SemaphoreType.DMA
     vmem = pl.BlockSpec(memory_space=pltpu.VMEM)
@@ -294,18 +335,18 @@
             pltpu.VMEM((n_j, n_y, width, LANES), bf16),
             pltpu.VMEM((n_j, width, LANES), bf16),
             pltpu.VMEM((n_z, width, LANES), bf16),
-            pltpu.VMEM((procs, half, LANES), bf16),
-            pltpu.VMEM((procs, half, LANES), bf16),
-            pltpu.VMEM((n_z, n_y, half, LANES), bf16),
-            pltpu.VMEM((n_y, half, LANES), bf16),
+            pltpu.VMEM((n_y * n_j, width, LANES), bf16),
+            pltpu.VMEM((n_y * n_j, width, LANES), bf16),
+            pltpu.VMEM((n_j, n_y, width, LANES), bf16),
+            pltpu.VMEM((n_y, width, LANES), bf16),
             pltpu.VMEM((n_c, share, rows), bf16),
             pltpu.VMEM((share, rows), bf16),
             pltpu.VMEM((width, width), jnp.float32),
             pltpu.VMEM((1, width), jnp.int32),
-            dma((3,)), dma((n_y,)), dma((n_j, n_y)), dma((n_j, n_y)), dma((n_z,)), dma((n_z,)),
-            dma((n_z,)), dma((1,)), dma((n_y,)), dma((1,)),
-            dma((n_z,)), dma((n_z,)), dma((n_z, n_y)), dma((procs,)),
-            dma((n_z,)), dma((n_z,)), dma((n_z, n_y)), dma((procs,)), dma((n_c,)), dma((n_c,)),
+            dma((3,)), dma((n_y,)), dma((n_j, n_y)), dma((n_j, n_y)), dma((n_j,)), dma((n_z,)),
+            dma((n_j,)), dma((1,)), dma((n_y,)), dma((1,)),
+            dma((n_z,)), dma((n_j,)), dma((n_j, n_y)), dma((n_y * n_j,)),
+            dma((n_z,)), dma((n_j,)), dma((n_j, n_y)), dma((n_y * n_j,)), dma((n_c,)), dma((n_c,)),
         ],
         compiler_params=pltpu.CompilerParams(
             collective_id=0, has_side_effects=True, vmem_limit_bytes=32 * 1024 * 1024

time: 38 us -> 36.6 us (0.963)
  Pallas kernels: 37.9 us -> 36.5 us
    pallas_call x1, Pallas kernels: 35.4 us -> 34 us  [shards(): pl.pallas_call(functools.partial(kernel, n_y, n_z, n_c, rows, cols, width...]
where the time goes in v3:
time: 36.6 us; the launch traced here: 36.5 us
  Pallas kernels  36.5 us (100%)
    pallas_call x1, Pallas kernels, shards(): pl.pallas_call(functools.partial(kernel, n_y, n_z, n_c, rows, cols, width...  34 us
    pallas_call x1, Pallas kernels, shards(): pl.pallas_call(functools.partial(update, parts), out_shape=jax.ShapeDtype...  2.51 us

profile of v3, /device:TPU:2, one launch (start us, length us, event | category | flops | bytes accessed | tf_op | source)
XLA Modules:
  0.0 36.5 jit_solution(12150439756757900657)
XLA Ops:
  0.0 34.0 %exchange.1 = (bf16[1024,2048]{1,0:T(8,128)(2,1)S(1)}, bf16[1024,256]{1,0:T(8,128)(2,1)S(1)}, bf16[256,2048]{1,0:T(8,128)(2,1)S(1)}) custom-call(bf16[1024,2048]{1,0:T(8,128)(2,1)} %trailing_ref.1, bf16[16,1024]{1,0:T(8,128)(2,1)} %bitcast.2, f32[128,128]{1,0:T(8,128)} %inverse_ref.1, s32[1,128]{1,0:T(1,128)} %bitcast.3), custom_call_target="tpu_custom_call" | custom-call | tf_op jit(solution)/shard_map/exchange/pallas_call | solution.py:325
  34.0 2.5 %update.1 = bf16[1024,2048]{1,0:T(8,128)(2,1)} custom-call(bf16[1024,2048]{1,0:T(8,128)(2,1)S(1)} %get-tuple-element.8.held, bf16[1024,256]{1,0:T(8,128)(2,1)S(1)} %get-tuple-element.9.left, bf16[256,2048]{1,0:T(8,128)(2,1)S(1)} %get-tuple-element.10.right), custom_call_target="tpu_custom_call" | custom-call | tf_op jit(solution)/shard_map/update/pallas_call | solution.py:360

commit v4 on v3

--- a/solution.py
+++ b/solution.py
@@ -137,21 +137,6 @@
         send(panel_held, panels.at[c], panel_send.at[k], panel_recv.at[k], me, ck)
     panels[c] = panel_held[...]
 
-    def spread_z(ref, send_sems, recv_sems):
-        for k in near_first(n_z):
-            send(ref.at[me], ref.at[me], send_sems.at[k], recv_sems.at[z], y * n_z + z_peer(k), c)
-
-    def hand_on(ref, send_sems, recv_sems, kz):
-        slot = y * n_z + z_peer(kz)
-        for k in far_first(n_y)[:-1]:
-            send(ref.at[slot], ref.at[slot], send_sems.at[kz, k], recv_sems.at[slot], y_peer(k) * n_z + z, c)
-
-    def hand_on_all(ref, z_sems, send_sems, recv_sems):
-        for kz in near_first(n_z):
-            zk = z_peer(kz)
-            arrived(ref.at[y * n_z + zk], z_sems.at[zk])
-            hand_on(ref, send_sems, recv_sems, kz)
-
     def top_along_y(k):
         return remote(top_in.at[k], top_all.at[k * n_j + j_own], spread_send.at[k], spread_recv.at[0],
                       k * n_z + z, c)
@@ -163,6 +148,8 @@
         for k in far_first(n_y)[:-1]:
             top_along_y(k).start()
         top_all[mine] = top_in[0]
+
+    pl.when(jnp.logical_and(y == 0, collects))(pass_top_on)
 
     def to_collector(m):
         j = (j_own + m) % n_j
@@ -180,8 +167,6 @@
             to_collector(m).start()
         else:
             pl.when(jnp.logical_not(collects))(lambda: to_collector(0).start())
-        if m == j_order[0]:
-            pl.when(jnp.logical_and(y == 0, collects))(pass_top_on)
 
     def along_z(ref, send_sems, recv_sems, k):
         return remote(ref.at[mine], ref.at[mine], send_sems.at[k], recv_sems.at[j_own], y * n_z + z_peer(k), c)
@@ -207,6 +192,14 @@
             else:
                 pl.when(jnp.logical_not(collects))(wait)
             hand_on(ref, send_sems, recv_sems, m)
+
+    @pl.when(collects)
+    def _():
+        @pl.when(y != 0)
+        def _():
+            arrived(top_all.at[mine], spread_recv.at[0])
+
+        spread_z(top_all, tz_send, tz_recv)
 
     tile = LANES
 
@@ -225,14 +218,6 @@
 
     lax.fori_loop(0, rows // tile, mask, 0)
 
-    @pl.when(collects)
-    def _():
-        @pl.when(y != 0)
-        def _():
-            arrived(top_all.at[mine], spread_recv.at[0])
-
-        spread_z(top_all, tz_send, tz_recv)
-
     small[2].wait()
 
     @pl.when(collects)
@@ -302,15 +287,15 @@
 
 
 def update(parts, held, left, right, out_ref, done, sems):
-    step = held.shape[1] // parts
+    step = held.shape[0] // parts
     for n in range(parts):
         span = slice(n * step, (n + 1) * step)
-        term = jnp.dot(left[...], right[:, span], preferred_element_type=jnp.float32)
-        done[n] = (held[:, span].astype(jnp.float32) + term).astype(jnp.bfloat16)
-        pltpu.make_async_copy(done.at[n], out_ref.at[:, span], sems.at[n]).start()
+        term = jnp.dot(left[span, :], right[...], preferred_element_type=jnp.float32)
+        done[n] = (held[span, :].astype(jnp.float32) + term).astype(jnp.bfloat16)
+        pltpu.make_async_copy(done.at[n], out_ref.at[span, :], sems.at[n]).start()
     for n in range(parts):
         span = slice(n * step, (n + 1) * step)
-        pltpu.make_async_copy(done.at[n], out_ref.at[:, span], sems.at[n]).wait()
+        pltpu.make_async_copy(done.at[n], out_ref.at[span, :], sems.at[n]).wait()
 
 
 def shards(trailing, panel_block, lower_inverse, pivot_pairs):
@@ -362,7 +347,7 @@
         out_shape=jax.ShapeDtypeStruct((rows, cols), bf16),
         in_specs=[vmem] * 3,
         out_specs=pl.BlockSpec(memory_space=pltpu.HBM),
-        scratch_shapes=[pltpu.VMEM((parts, rows, cols // parts), bf16), dma((parts,))],
+        scratch_shapes=[pltpu.VMEM((parts, rows // parts, cols), bf16), dma((parts,))],
         compiler_params=pltpu.CompilerParams(vmem_limit_bytes=32 * 1024 * 1024),
         name="update",
     )(*(pltpu.with_memory_space_constraint(value, pltpu.VMEM) for value in factors))

time: 36.6 us -> 36.5 us (level)
  no operation moved by 1% of the time
where the time goes in v4:
time: 36.5 us; the launch traced here: 36.4 us
  Pallas kernels  36.4 us (100%)
    pallas_call x1, Pallas kernels, shards(): pl.pallas_call(functools.partial(kernel, n_y, n_z, n_c, rows, cols, width...  34 us
    pallas_call x1, Pallas kernels, shards(): pl.pallas_call(functools.partial(update, parts), out_shape=jax.ShapeDtype...  2.39 us

profile of v4, /device:TPU:2, one launch (start us, length us, event | category | flops | bytes accessed | tf_op | source)
XLA Modules:
  0.0 36.4 jit_solution(7350929116880443417)
XLA Ops:
  0.0 34.0 %exchange.1 = (bf16[1024,2048]{1,0:T(8,128)(2,1)S(1)}, bf16[1024,256]{1,0:T(8,128)(2,1)S(1)}, bf16[256,2048]{1,0:T(8,128)(2,1)S(1)}) custom-call(bf16[1024,2048]{1,0:T(8,128)(2,1)} %trailing_ref.1, bf16[16,1024]{1,0:T(8,128)(2,1)} %bitcast.2, f32[128,128]{1,0:T(8,128)} %inverse_ref.1, s32[1,128]{1,0:T(1,128)} %bitcast.3), custom_call_target="tpu_custom_call" | custom-call | tf_op jit(solution)/shard_map/exchange/pallas_call | solution.py:310
  34.0 2.4 %update.1 = bf16[1024,2048]{1,0:T(8,128)(2,1)} custom-call(bf16[1024,2048]{1,0:T(8,128)(2,1)S(1)} %get-tuple-element.8.held, bf16[1024,256]{1,0:T(8,128)(2,1)S(1)} %get-tuple-element.9.left, bf16[256,2048]{1,0:T(8,128)(2,1)S(1)} %get-tuple-element.10.right), custom_call_target="tpu_custom_call" | custom-call | tf_op jit(solution)/shard_map/update/pallas_call | solution.py:345

commit v5 on v4

--- a/solution.py
+++ b/solution.py
@@ -218,6 +218,8 @@
 
     lax.fori_loop(0, rows // tile, mask, 0)
 
+    hand_on_all(top_all, tz_recv, ty_send, ty_recv, [0])
+
     small[2].wait()
 
     @pl.when(collects)
@@ -232,7 +234,7 @@
         u_all[mine] = u.astype(bf16)
         spread_z(u_all, uz_send, uz_recv)
 
-    hand_on_all(top_all, tz_recv, ty_send, ty_recv, [0, 1])
+    hand_on_all(top_all, tz_recv, ty_send, ty_recv, [1, 3])
 
     for k in range(1, n_c):
         arrived(panels.at[(c + n_c - k) % n_c], panel_recv.at[k])
@@ -246,7 +248,6 @@
         left[0:width, 0:width] = (row == col).astype(bf16)
 
     hand_on_all(u_all, uz_recv, uy_send, uy_recv, [0])
-    hand_on_all(top_all, tz_recv, ty_send, ty_recv, [3])
     hand_on_all(u_all, uz_recv, uy_send, uy_recv, [1])
     hand_on_all(top_all, tz_recv, ty_send, ty_recv, [2])
     hand_on_all(u_all, uz_recv, uy_send, uy_recv, [3, 2])

time: 36.5 us -> 36.1 us (0.989)
  Pallas kernels: 36.4 us -> 35.9 us
    pallas_call x1, Pallas kernels: 34 us -> 33.5 us  [shards(): pl.pallas_call(functools.partial(kernel, n_y, n_z, n_c, rows, cols, width...]
where the time goes in v5:
time: 36.1 us; the launch traced here: 35.9 us
  Pallas kernels  35.9 us (99%)
    pallas_call x1, Pallas kernels, shards(): pl.pallas_call(functools.partial(kernel, n_y, n_z, n_c, rows, cols, width...  33.5 us
    pallas_call x1, Pallas kernels, shards(): pl.pallas_call(functools.partial(update, parts), out_shape=jax.ShapeDtype...  2.39 us

profile of v5, /device:TPU:2, one launch (start us, length us, event | category | flops | bytes accessed | tf_op | source)
XLA Modules:
  0.0 35.9 jit_solution(14441238075052302845)
XLA Ops:
  0.0 33.5 %exchange.1 = (bf16[1024,2048]{1,0:T(8,128)(2,1)S(1)}, bf16[1024,256]{1,0:T(8,128)(2,1)S(1)}, bf16[256,2048]{1,0:T(8,128)(2,1)S(1)}) custom-call(bf16[1024,2048]{1,0:T(8,128)(2,1)} %trailing_ref.1, bf16[16,1024]{1,0:T(8,128)(2,1)} %bitcast.2, f32[128,128]{1,0:T(8,128)} %inverse_ref.1, s32[1,128]{1,0:T(1,128)} %bitcast.3), custom_call_target="tpu_custom_call" | custom-call | tf_op jit(solution)/shard_map/exchange/pallas_call | solution.py:311
  33.5 2.4 %update.1 = bf16[1024,2048]{1,0:T(8,128)(2,1)} custom-call(bf16[1024,2048]{1,0:T(8,128)(2,1)S(1)} %get-tuple-element.8.held, bf16[1024,256]{1,0:T(8,128)(2,1)S(1)} %get-tuple-element.9.left, bf16[256,2048]{1,0:T(8,128)(2,1)S(1)} %get-tuple-element.10.right), custom_call_target="tpu_custom_call" | custom-call | tf_op jit(solution)/shard_map/update/pallas_call | solution.py:346
